TPU v7x, 128 devices: a whole 4x4x4 slice. The times are simulated.
128 devices in a mesh: seq: 16 (over x_hi, y, core), chan: 8 (over x_lo, z).
Axes of the slice: x: 4 (x_hi: 2, x_lo: 2; x = x_hi * 2 + x_lo), y: 4, z: 4, core: 2. Of those that a mesh axis runs over, the one named last changes fastest.
Arguments:
- out_gate: bfloat16 [4096, 8192], P('seq', 'chan'), may hold values from -6 to 6
- in_gate: bfloat16 [4096, 8192], P('seq', 'chan'), may hold values from -6 to 6
- signal: bfloat16 [4096, 8192], P('seq', 'chan'), may hold values from -6 to 6
- filter_taps: bfloat16 [4096, 8192], P('seq', 'chan'), may hold values from -5 to 5
- skip_gain: float32 [8192], P('chan'), may hold values from -4 to 4
- out_proj: bfloat16 [8192, 8192], P(None, 'chan'), may hold values from -0.09375 to 0.09375
Outputs:
- layer_out: bfloat16 [4096, 8192], P('seq', 'chan')
All inputs are finite; a program needn't handle non-finite values.
Results may differ from a plain program's by a relative error of at most 0.02.
Values may be sent and summed in bfloat16 or wider, within the bound.
No kernel may reach another device: no remote copies, remote signals or barrier semaphores. Data moves between devices by JAX's collectives and lax.ppermute only.
A program may use at most 128 MiB of HBM per device.

v0:
```python
import math
import jax
import jax.numpy as jnp
from jax import lax
from jax.sharding import PartitionSpec as P


def passed_along(block, axis, distance):
    devices = range(lax.axis_size(axis))
    route = [(i - distance, i) for i in devices if i - distance in devices]
    return lax.ppermute(block, axis, route)


def fourier_tables(block_len):
    length = 2 * block_len
    freq_index = jnp.arange(block_len, dtype=jnp.int32)[:, None]
    moment = jnp.arange(block_len, dtype=jnp.int32)[None, :]
    angle_table = 2.0 * math.pi / length * (freq_index * moment % length).astype(jnp.float32)
    alternate = jnp.where(moment % 2 == 0, 1.0, -1.0).astype(jnp.float32)
    cosine = jnp.cos(angle_table)
    sine_table = jnp.sin(angle_table)
    forward_imag = jnp.where(freq_index == 0, alternate, -sine_table)
    forward = jnp.concatenate([cosine, forward_imag], axis=0)
    weight = jnp.where(moment == 0, 1.0, 2.0).astype(jnp.float32) / length
    inverse_real = cosine * weight
    inverse_imag = jnp.where(moment == 0, alternate.T / length, -2.0 / length * sine_table)
    inverse = jnp.concatenate([inverse_real, inverse_imag], axis=1)
    keep_mask = (jnp.arange(block_len) > 0).astype(jnp.float32)
    sign_half = jnp.where(jnp.arange(block_len) % 2 == 0, 1.0, -1.0).astype(jnp.float32)
    sign_pattern = jnp.concatenate([sign_half, sign_half])
    forward_high = forward.astype(jnp.bfloat16)
    forward_low = (forward - forward_high.astype(jnp.float32)).astype(jnp.bfloat16)
    return ((forward_high, forward_low), inverse, keep_mask, sign_pattern)


def spectral_product(factor_left, factor_right, keep_mask, split_axis):
    left_real, left_imag = jnp.split(factor_left, 2, axis=split_axis)
    right_real, right_imag = jnp.split(factor_right, 2, axis=split_axis)
    cross_term = left_imag * right_imag
    real_part = left_real * right_real - keep_mask * cross_term
    imag_part = (
        keep_mask * (left_real * right_imag + left_imag * right_real)
        + (1.0 - keep_mask) * cross_term
    )
    return jnp.concatenate([real_part, imag_part], axis=split_axis)


def transform(tables, time_rows):
    first = jnp.dot(tables[0], time_rows, preferred_element_type=jnp.float32)
    return first + jnp.dot(tables[1], time_rows, preferred_element_type=jnp.float32)


def shards(out_gate, in_gate, signal, filter_taps, skip_gain, out_proj):
    block_len = out_gate.shape[0]
    seq_count = lax.axis_size("seq")
    highest = lax.Precision.HIGHEST
    gated_rows = (in_gate.astype(jnp.float32) * signal.astype(jnp.float32)).astype(jnp.bfloat16)
    tables, inverse, keep_mask, sign_pattern = fourier_tables(block_len)
    all_taps = lax.all_gather(filter_taps, "seq", axis=0, tiled=True)
    keep_col = keep_mask[:, None]
    sign_col = sign_pattern[:, None]

    def lag_spectrum(lag_index):
        return transform(
            tables, lax.dynamic_slice_in_dim(all_taps, lag_index * block_len, block_len, 0)
        )

    first_spec = lag_spectrum(0)
    running = spectral_product(first_spec, transform(tables, gated_rows), keep_col, 0)

    def add_source(lag_index, carry):
        running_sum, previous, held_rows = carry
        held_rows = passed_along(held_rows, "seq", 1)
        current = lag_spectrum(lag_index)
        pair_spec = current + sign_col * previous
        running_sum = running_sum + spectral_product(
            pair_spec, transform(tables, held_rows), keep_col, 0
        )
        return (running_sum, current, held_rows)

    running, last_spec, last_held = lax.fori_loop(
        1, seq_count, add_source, (running, first_spec, gated_rows)
    )
    conv_rows = jnp.dot(inverse, running, precision=highest)
    mixed_rows = (
        out_gate.astype(jnp.float32)
        * (conv_rows + skip_gain[None, :] * gated_rows.astype(jnp.float32))
    ).astype(jnp.bfloat16)
    summed = lax.psum_scatter(
        lax.dot_general(
            out_proj, mixed_rows, (((1,), (1,)), ((), ())), preferred_element_type=jnp.float32
        ).astype(jnp.bfloat16),
        "chan",
        scatter_dimension=0,
        tiled=True,
    ).astype(jnp.float32)
    return summed.T.astype(jnp.bfloat16)


def solution(mesh):
    return jax.shard_map(
        shards,
        mesh=mesh,
        in_specs=(
            P("seq", "chan"),
            P("seq", "chan"),
            P("seq", "chan"),
            P("seq", "chan"),
            P("chan"),
            P(None, "chan"),
        ),
        out_specs=P("seq", "chan"),
        check_vma=False,
    )
```

profile of v0, /device:TPU:1, one launch (start us, length us, event | category | flops | bytes accessed | tf_op | source)
XLA Modules:
  0.0 416.8 jit_solution(1783234137124301524)
XLA Ops:
  14.4 72.0 %all-gather.2.cloned.1.call-done = bf16[4096,1024]{1,0:T(8,128)(2,1)} async-done(((bf16[256,1024]{1,0:T(8,128)(2,1)}), bf16[4096,1024]{1,0:T(8,128)(2,1)}) %all-gather.2.cloned.1.call-update) | async-done | bytes 8388624 | tf_op jit(solution)/shard_map/all_gather | solution.py:59
  90.9 212.7 %while.19 = (s32[]{:T(128)}, f32[512,1024]{1,0:T(8,128)S(1)}, f32[512,1024]{1,0:T(8,128)}, bf16[256,1024]{1,0:T(8,128)(2,1)}, bf16[4096,1024]{1,0:T(8,128)(2,1)}...) while((s32[]{:T(128)}, f32[512,1024]{1,0:T(8,128)S(1)}, ...), condition=%wide.region_1.2_spmd.clone.clone, body=%wide.region_0.1_spmd.clone.clone.sunk | while | flops 1079509760 | bytes 52436232 | solution.py:81
  102.2 4.3 %collective-permute-start = (bf16[256,1024]{1,0:T(8,128)(2,1)}, bf16[256,1024]{1,0:T(8,128)(2,1)S(1)}, u32[]{:S(2)}, u32[]{:S(2)}) collective-permute-start(bf16[256,1024]{1,0:T(8,128)(2,1)} %get-tuple-element.307), channel_id=1, source_target_pairs={{0,8},{8,16},{16,24},{24,32},{32,40},{40,48},{48,56},{56,64},{64,7... | collective-permute-start | bytes 1572872 | tf_op jit(solution)/shard_map/while/body/eval_jaxpr/ppermute | solution.py:11
  110.4 2.6 collective-permute-done
  115.7 4.3 %collective-permute-start = (bf16[256,1024]{1,0:T(8,128)(2,1)}, bf16[256,1024]{1,0:T(8,128)(2,1)S(1)}, u32[]{:S(2)}, u32[]{:S(2)}) collective-permute-start(bf16[256,1024]{1,0:T(8,128)(2,1)} %get-tuple-element.307), channel_id=1, source_target_pairs={{0,8},{8,16},{16,24},{24,32},{32,40},{40,48},{48,56},{56,64},{64,7... | collective-permute-start | bytes 1572872 | tf_op jit(solution)/shard_map/while/body/eval_jaxpr/ppermute | solution.py:11
  123.8 2.6 collective-permute-done
  129.2 4.3 %collective-permute-start = (bf16[256,1024]{1,0:T(8,128)(2,1)}, bf16[256,1024]{1,0:T(8,128)(2,1)S(1)}, u32[]{:S(2)}, u32[]{:S(2)}) collective-permute-start(bf16[256,1024]{1,0:T(8,128)(2,1)} %get-tuple-element.307), channel_id=1, source_target_pairs={{0,8},{8,16},{16,24},{24,32},{32,40},{40,48},{48,56},{56,64},{64,7... | collective-permute-start | bytes 1572872 | tf_op jit(solution)/shard_map/while/body/eval_jaxpr/ppermute | solution.py:11
  142.6 4.3 %collective-permute-start = (bf16[256,1024]{1,0:T(8,128)(2,1)}, bf16[256,1024]{1,0:T(8,128)(2,1)S(1)}, u32[]{:S(2)}, u32[]{:S(2)}) collective-permute-start(bf16[256,1024]{1,0:T(8,128)(2,1)} %get-tuple-element.307), channel_id=1, source_target_pairs={{0,8},{8,16},{16,24},{24,32},{32,40},{40,48},{48,56},{56,64},{64,7... | collective-permute-start | bytes 1572872 | tf_op jit(solution)/shard_map/while/body/eval_jaxpr/ppermute | solution.py:11
  156.1 4.3 %collective-permute-start = (bf16[256,1024]{1,0:T(8,128)(2,1)}, bf16[256,1024]{1,0:T(8,128)(2,1)S(1)}, u32[]{:S(2)}, u32[]{:S(2)}) collective-permute-start(bf16[256,1024]{1,0:T(8,128)(2,1)} %get-tuple-element.307), channel_id=1, source_target_pairs={{0,8},{8,16},{16,24},{24,32},{32,40},{40,48},{48,56},{56,64},{64,7... | collective-permute-start | bytes 1572872 | tf_op jit(solution)/shard_map/while/body/eval_jaxpr/ppermute | solution.py:11
  169.5 4.3 %collective-permute-start = (bf16[256,1024]{1,0:T(8,128)(2,1)}, bf16[256,1024]{1,0:T(8,128)(2,1)S(1)}, u32[]{:S(2)}, u32[]{:S(2)}) collective-permute-start(bf16[256,1024]{1,0:T(8,128)(2,1)} %get-tuple-element.307), channel_id=1, source_target_pairs={{0,8},{8,16},{16,24},{24,32},{32,40},{40,48},{48,56},{56,64},{64,7... | collective-permute-start | bytes 1572872 | tf_op jit(solution)/shard_map/while/body/eval_jaxpr/ppermute | solution.py:11
  183.0 4.3 %collective-permute-start = (bf16[256,1024]{1,0:T(8,128)(2,1)}, bf16[256,1024]{1,0:T(8,128)(2,1)S(1)}, u32[]{:S(2)}, u32[]{:S(2)}) collective-permute-start(bf16[256,1024]{1,0:T(8,128)(2,1)} %get-tuple-element.307), channel_id=1, source_target_pairs={{0,8},{8,16},{16,24},{24,32},{32,40},{40,48},{48,56},{56,64},{64,7... | collective-permute-start | bytes 1572872 | tf_op jit(solution)/shard_map/while/body/eval_jaxpr/ppermute | solution.py:11
  196.4 4.3 %collective-permute-start = (bf16[256,1024]{1,0:T(8,128)(2,1)}, bf16[256,1024]{1,0:T(8,128)(2,1)S(1)}, u32[]{:S(2)}, u32[]{:S(2)}) collective-permute-start(bf16[256,1024]{1,0:T(8,128)(2,1)} %get-tuple-element.307), channel_id=1, source_target_pairs={{0,8},{8,16},{16,24},{24,32},{32,40},{40,48},{48,56},{56,64},{64,7... | collective-permute-start | bytes 1572872 | tf_op jit(solution)/shard_map/while/body/eval_jaxpr/ppermute | solution.py:11
  209.9 4.3 %collective-permute-start = (bf16[256,1024]{1,0:T(8,128)(2,1)}, bf16[256,1024]{1,0:T(8,128)(2,1)S(1)}, u32[]{:S(2)}, u32[]{:S(2)}) collective-permute-start(bf16[256,1024]{1,0:T(8,128)(2,1)} %get-tuple-element.307), channel_id=1, source_target_pairs={{0,8},{8,16},{16,24},{24,32},{32,40},{40,48},{48,56},{56,64},{64,7... | collective-permute-start | bytes 1572872 | tf_op jit(solution)/shard_map/while/body/eval_jaxpr/ppermute | solution.py:11
  218.0 2.6 collective-permute-done
  223.4 4.3 %collective-permute-start = (bf16[256,1024]{1,0:T(8,128)(2,1)}, bf16[256,1024]{1,0:T(8,128)(2,1)S(1)}, u32[]{:S(2)}, u32[]{:S(2)}) collective-permute-start(bf16[256,1024]{1,0:T(8,128)(2,1)} %get-tuple-element.307), channel_id=1, source_target_pairs={{0,8},{8,16},{16,24},{24,32},{32,40},{40,48},{48,56},{56,64},{64,7... | collective-permute-start | bytes 1572872 | tf_op jit(solution)/shard_map/while/body/eval_jaxpr/ppermute | solution.py:11
  231.5 2.6 collective-permute-done
  236.8 6.5 %collective-permute-start = (bf16[256,1024]{1,0:T(8,128)(2,1)}, bf16[256,1024]{1,0:T(8,128)(2,1)S(1)}, u32[]{:S(2)}, u32[]{:S(2)}) collective-permute-start(bf16[256,1024]{1,0:T(8,128)(2,1)} %get-tuple-element.307), channel_id=1, source_target_pairs={{0,8},{8,16},{16,24},{24,32},{32,40},{40,48},{48,56},{56,64},{64,7... | collective-permute-start | bytes 1572872 | tf_op jit(solution)/shard_map/while/body/eval_jaxpr/ppermute | solution.py:11
  247.2 2.6 collective-permute-done
  252.5 7.9 %collective-permute-start = (bf16[256,1024]{1,0:T(8,128)(2,1)}, bf16[256,1024]{1,0:T(8,128)(2,1)S(1)}, u32[]{:S(2)}, u32[]{:S(2)}) collective-permute-start(bf16[256,1024]{1,0:T(8,128)(2,1)} %get-tuple-element.307), channel_id=1, source_target_pairs={{0,8},{8,16},{16,24},{24,32},{32,40},{40,48},{48,56},{56,64},{64,7... | collective-permute-start | bytes 1572872 | tf_op jit(solution)/shard_map/while/body/eval_jaxpr/ppermute | solution.py:11
  269.5 7.9 %collective-permute-start = (bf16[256,1024]{1,0:T(8,128)(2,1)}, bf16[256,1024]{1,0:T(8,128)(2,1)S(1)}, u32[]{:S(2)}, u32[]{:S(2)}) collective-permute-start(bf16[256,1024]{1,0:T(8,128)(2,1)} %get-tuple-element.307), channel_id=1, source_target_pairs={{0,8},{8,16},{16,24},{24,32},{32,40},{40,48},{48,56},{56,64},{64,7... | collective-permute-start | bytes 1572872 | tf_op jit(solution)/shard_map/while/body/eval_jaxpr/ppermute | solution.py:11
  286.6 7.9 %collective-permute-start = (bf16[256,1024]{1,0:T(8,128)(2,1)}, bf16[256,1024]{1,0:T(8,128)(2,1)S(1)}, u32[]{:S(2)}, u32[]{:S(2)}) collective-permute-start(bf16[256,1024]{1,0:T(8,128)(2,1)} %get-tuple-element.307), channel_id=1, source_target_pairs={{0,8},{8,16},{16,24},{24,32},{32,40},{40,48},{48,56},{56,64},{64,7... | collective-permute-start | bytes 1572872 | tf_op jit(solution)/shard_map/while/body/eval_jaxpr/ppermute | solution.py:11
  303.7 3.2 fusion.9
  306.9 9.5 %fusion.7 = bf16[8192,256]{0,1:T(8,128)(2,1)} fusion(bf16[256,1024]{1,0:T(8,128)(2,1)S(1)} %fusion.9, bf16[8192,1024]{1,0:T(8,128)(2,1)} %param.13), kind=kOutput, calls=%fused_computation.16 | convolution fusion | flops 4297064448 | bytes 21495808 | tf_op jit(solution)/shard_map/dot_general | solution.py:90
  316.4 93.6 %reduce-scatter.2.cloned.1.call-done = bf16[1024,256]{0,1:T(8,128)(2,1)} async-done(((bf16[8192,256]{0,1:T(8,128)(2,1)}), bf16[1024,256]{0,1:T(8,128)(2,1)}) %reduce-scatter.2.cloned.1.call-update) | async-done | bytes 524304 | tf_op jit(solution)/shard_map/reduce_scatter | solution.py:89
  (234 shorter events, 137.8 us)
Async XLA Ops:
  6.5 79.8 %all-gather.2.cloned.1.call-start = ((), (), s32[]{:S(2)}) async-start(), calls=%async_computation.1 | async-start | bytes 8912896 | tf_op jit(solution)/shard_map/all_gather | solution.py:59
  7.3 402.7 %reduce-scatter.2.cloned.1.call-start = ((), (), s32[]{:S(2)}) async-start(), calls=%async_computation.2 | async-start | bytes 4718592 | tf_op jit(solution)/shard_map/reduce_scatter | solution.py:89
  8.8 5.1 %copy-start.3 = (bf16[256,1024]{1,0:T(8,128)(2,1)}, bf16[256,1024]{1,0:T(8,128)(2,1)S(1)}, u32[]{:S(2)}) copy-start(bf16[256,1024]{1,0:T(8,128)(2,1)S(1)} %multiply_convert_fusion) | copy-start | bytes 1572868
  90.9 212.8 %copy-start.4 = (f32[1024]{0:T(1024)S(1)}, f32[1024]{0:T(1024)}, u32[]{:S(2)}) copy-start(f32[1024]{0:T(1024)} %param.12) | copy-start | bytes 12292
  91.1 8.4 %collective-permute-start = (bf16[256,1024]{1,0:T(8,128)(2,1)}, bf16[256,1024]{1,0:T(8,128)(2,1)S(1)}, u32[]{:S(2)}, u32[]{:S(2)}) collective-permute-start(bf16[256,1024]{1,0:T(8,128)(2,1)} %get-tuple-element.307), channel_id=1, source_target_pairs={{0,8},{8,16},{16,24},{24,32},{32,40},{40,48},{48,56},{56,64},{64,7... | collective-permute-start | bytes 1572872 | tf_op jit(solution)/shard_map/while/body/eval_jaxpr/ppermute | solution.py:11
  96.9 3.5 copy-start.2
  102.2 10.7 %collective-permute-start = (bf16[256,1024]{1,0:T(8,128)(2,1)}, bf16[256,1024]{1,0:T(8,128)(2,1)S(1)}, u32[]{:S(2)}, u32[]{:S(2)}) collective-permute-start(bf16[256,1024]{1,0:T(8,128)(2,1)} %get-tuple-element.307), channel_id=1, source_target_pairs={{0,8},{8,16},{16,24},{24,32},{32,40},{40,48},{48,56},{56,64},{64,7... | collective-permute-start | bytes 1572872 | tf_op jit(solution)/shard_map/while/body/eval_jaxpr/ppermute | solution.py:11
  110.4 3.5 copy-start.2
  115.7 10.7 %collective-permute-start = (bf16[256,1024]{1,0:T(8,128)(2,1)}, bf16[256,1024]{1,0:T(8,128)(2,1)S(1)}, u32[]{:S(2)}, u32[]{:S(2)}) collective-permute-start(bf16[256,1024]{1,0:T(8,128)(2,1)} %get-tuple-element.307), channel_id=1, source_target_pairs={{0,8},{8,16},{16,24},{24,32},{32,40},{40,48},{48,56},{56,64},{64,7... | collective-permute-start | bytes 1572872 | tf_op jit(solution)/shard_map/while/body/eval_jaxpr/ppermute | solution.py:11
  123.8 3.5 copy-start.2
  129.2 10.7 %collective-permute-start = (bf16[256,1024]{1,0:T(8,128)(2,1)}, bf16[256,1024]{1,0:T(8,128)(2,1)S(1)}, u32[]{:S(2)}, u32[]{:S(2)}) collective-permute-start(bf16[256,1024]{1,0:T(8,128)(2,1)} %get-tuple-element.307), channel_id=1, source_target_pairs={{0,8},{8,16},{16,24},{24,32},{32,40},{40,48},{48,56},{56,64},{64,7... | collective-permute-start | bytes 1572872 | tf_op jit(solution)/shard_map/while/body/eval_jaxpr/ppermute | solution.py:11
  142.6 10.7 %collective-permute-start = (bf16[256,1024]{1,0:T(8,128)(2,1)}, bf16[256,1024]{1,0:T(8,128)(2,1)S(1)}, u32[]{:S(2)}, u32[]{:S(2)}) collective-permute-start(bf16[256,1024]{1,0:T(8,128)(2,1)} %get-tuple-element.307), channel_id=1, source_target_pairs={{0,8},{8,16},{16,24},{24,32},{32,40},{40,48},{48,56},{56,64},{64,7... | collective-permute-start | bytes 1572872 | tf_op jit(solution)/shard_map/while/body/eval_jaxpr/ppermute | solution.py:11
  156.1 10.7 %collective-permute-start = (bf16[256,1024]{1,0:T(8,128)(2,1)}, bf16[256,1024]{1,0:T(8,128)(2,1)S(1)}, u32[]{:S(2)}, u32[]{:S(2)}) collective-permute-start(bf16[256,1024]{1,0:T(8,128)(2,1)} %get-tuple-element.307), channel_id=1, source_target_pairs={{0,8},{8,16},{16,24},{24,32},{32,40},{40,48},{48,56},{56,64},{64,7... | collective-permute-start | bytes 1572872 | tf_op jit(solution)/shard_map/while/body/eval_jaxpr/ppermute | solution.py:11
  169.5 10.7 %collective-permute-start = (bf16[256,1024]{1,0:T(8,128)(2,1)}, bf16[256,1024]{1,0:T(8,128)(2,1)S(1)}, u32[]{:S(2)}, u32[]{:S(2)}) collective-permute-start(bf16[256,1024]{1,0:T(8,128)(2,1)} %get-tuple-element.307), channel_id=1, source_target_pairs={{0,8},{8,16},{16,24},{24,32},{32,40},{40,48},{48,56},{56,64},{64,7... | collective-permute-start | bytes 1572872 | tf_op jit(solution)/shard_map/while/body/eval_jaxpr/ppermute | solution.py:11
  183.0 10.7 %collective-permute-start = (bf16[256,1024]{1,0:T(8,128)(2,1)}, bf16[256,1024]{1,0:T(8,128)(2,1)S(1)}, u32[]{:S(2)}, u32[]{:S(2)}) collective-permute-start(bf16[256,1024]{1,0:T(8,128)(2,1)} %get-tuple-element.307), channel_id=1, source_target_pairs={{0,8},{8,16},{16,24},{24,32},{32,40},{40,48},{48,56},{56,64},{64,7... | collective-permute-start | bytes 1572872 | tf_op jit(solution)/shard_map/while/body/eval_jaxpr/ppermute | solution.py:11
  191.1 3.5 copy-start.2
  196.4 10.7 %collective-permute-start = (bf16[256,1024]{1,0:T(8,128)(2,1)}, bf16[256,1024]{1,0:T(8,128)(2,1)S(1)}, u32[]{:S(2)}, u32[]{:S(2)}) collective-permute-start(bf16[256,1024]{1,0:T(8,128)(2,1)} %get-tuple-element.307), channel_id=1, source_target_pairs={{0,8},{8,16},{16,24},{24,32},{32,40},{40,48},{48,56},{56,64},{64,7... | collective-permute-start | bytes 1572872 | tf_op jit(solution)/shard_map/while/body/eval_jaxpr/ppermute | solution.py:11
  204.6 3.5 copy-start.2
  209.9 10.7 %collective-permute-start = (bf16[256,1024]{1,0:T(8,128)(2,1)}, bf16[256,1024]{1,0:T(8,128)(2,1)S(1)}, u32[]{:S(2)}, u32[]{:S(2)}) collective-permute-start(bf16[256,1024]{1,0:T(8,128)(2,1)} %get-tuple-element.307), channel_id=1, source_target_pairs={{0,8},{8,16},{16,24},{24,32},{32,40},{40,48},{48,56},{56,64},{64,7... | collective-permute-start | bytes 1572872 | tf_op jit(solution)/shard_map/while/body/eval_jaxpr/ppermute | solution.py:11
  223.4 10.7 %collective-permute-start = (bf16[256,1024]{1,0:T(8,128)(2,1)}, bf16[256,1024]{1,0:T(8,128)(2,1)S(1)}, u32[]{:S(2)}, u32[]{:S(2)}) collective-permute-start(bf16[256,1024]{1,0:T(8,128)(2,1)} %get-tuple-element.307), channel_id=1, source_target_pairs={{0,8},{8,16},{16,24},{24,32},{32,40},{40,48},{48,56},{56,64},{64,7... | collective-permute-start | bytes 1572872 | tf_op jit(solution)/shard_map/while/body/eval_jaxpr/ppermute | solution.py:11
  236.8 12.9 %collective-permute-start = (bf16[256,1024]{1,0:T(8,128)(2,1)}, bf16[256,1024]{1,0:T(8,128)(2,1)S(1)}, u32[]{:S(2)}, u32[]{:S(2)}) collective-permute-start(bf16[256,1024]{1,0:T(8,128)(2,1)} %get-tuple-element.307), channel_id=1, source_target_pairs={{0,8},{8,16},{16,24},{24,32},{32,40},{40,48},{48,56},{56,64},{64,7... | collective-permute-start | bytes 1572872 | tf_op jit(solution)/shard_map/while/body/eval_jaxpr/ppermute | solution.py:11
  252.5 14.3 %collective-permute-start = (bf16[256,1024]{1,0:T(8,128)(2,1)}, bf16[256,1024]{1,0:T(8,128)(2,1)S(1)}, u32[]{:S(2)}, u32[]{:S(2)}) collective-permute-start(bf16[256,1024]{1,0:T(8,128)(2,1)} %get-tuple-element.307), channel_id=1, source_target_pairs={{0,8},{8,16},{16,24},{24,32},{32,40},{40,48},{48,56},{56,64},{64,7... | collective-permute-start | bytes 1572872 | tf_op jit(solution)/shard_map/while/body/eval_jaxpr/ppermute | solution.py:11
  269.5 14.3 %collective-permute-start = (bf16[256,1024]{1,0:T(8,128)(2,1)}, bf16[256,1024]{1,0:T(8,128)(2,1)S(1)}, u32[]{:S(2)}, u32[]{:S(2)}) collective-permute-start(bf16[256,1024]{1,0:T(8,128)(2,1)} %get-tuple-element.307), channel_id=1, source_target_pairs={{0,8},{8,16},{16,24},{24,32},{32,40},{40,48},{48,56},{56,64},{64,7... | collective-permute-start | bytes 1572872 | tf_op jit(solution)/shard_map/while/body/eval_jaxpr/ppermute | solution.py:11
  286.6 14.3 %collective-permute-start = (bf16[256,1024]{1,0:T(8,128)(2,1)}, bf16[256,1024]{1,0:T(8,128)(2,1)S(1)}, u32[]{:S(2)}, u32[]{:S(2)}) collective-permute-start(bf16[256,1024]{1,0:T(8,128)(2,1)} %get-tuple-element.307), channel_id=1, source_target_pairs={{0,8},{8,16},{16,24},{24,32},{32,40},{40,48},{48,56},{56,64},{64,7... | collective-permute-start | bytes 1572872 | tf_op jit(solution)/shard_map/while/body/eval_jaxpr/ppermute | solution.py:11
  (26 other events, 62.6 us)
Sparse Core Ops, SparseCore 0:
  9.8 76.4 all-gather.1
  316.5 93.4 reduce-scatter.1
where the time goes:
time: 419 us; the launch traced here: 417 us
  waiting for transfers between devices  205 us (49%)
  matrix products  85.6 us (20%)
  starting transfers between devices  74.8 us (18%)
  other arithmetic  21.4 us (5%)
  local copies, waits for them, and re-layouts  15.1 us (4%)
  between operations  13.5 us (3%)
    reduce_scatter x1, waiting for transfers between devices, shards(): lax.psum_scatter(lax.dot_general(out_proj, mixed_rows, (((1,), (1,)), (()...  93.6 us
    ppermute x15, starting transfers between devices, passed_along(): return lax.ppermute(block, axis, route)  74.8 us
    all_gather x1, waiting for transfers between devices, shards(): all_taps = lax.all_gather(filter_taps, 'seq', axis=0, tiled=True)  72 us
    dot_general x32, matrix products, transform(): jnp.dot(tables[1], time_rows, preferred_element_type=jnp.float32)  39.5 us
    ppermute x15, waiting for transfers between devices, passed_along(): return lax.ppermute(block, axis, route)  38.5 us
    dot_general x32, matrix products, transform(): first = jnp.dot(tables[0], time_rows, preferred_element_type=jnp.float32)  33.4 us
    while x75, local copies, waits for them, and re-layouts  13.4 us
    dot_general x1, matrix products, shards(): lax.dot_general(out_proj, mixed_rows, (((1,), (1,)), ((), ())), preferred...  9.48 us
  transfers between devices with their start and end apart: 17, of which 17 were waited for; matrix products, arithmetic and copies ran while one was open for 15% of the time, Pallas kernels for 0%

commit v1 on v0

--- a/solution.py
+++ b/solution.py
@@ -56,7 +56,9 @@
     highest = lax.Precision.HIGHEST
     gated_rows = (in_gate.astype(jnp.float32) * signal.astype(jnp.float32)).astype(jnp.bfloat16)
     tables, inverse, keep_mask, sign_pattern = fourier_tables(block_len)
-    all_taps = lax.all_gather(filter_taps, "seq", axis=0, tiled=True)
+    all_taps = jnp.concatenate(
+        lax.all_to_all(jnp.stack([filter_taps] * lax.axis_size("seq")), "seq", 0, 0), axis=0
+    )
     keep_col = keep_mask[:, None]
     sign_col = sign_pattern[:, None]
 

time: 419 us -> 482 us (1.15)
  waiting for transfers between devices: 205 us -> 249 us
  starting transfers between devices: 74.8 us -> 89.7 us
  local copies, waits for them, and re-layouts: 15.1 us -> 20.5 us
    all_to_all x0 -> x1, waiting for transfers between devices: none -> 114 us  [shards(): lax.all_to_all(jnp.stack([filter_taps] * lax.axis_size('seq')), 'seq', 0, 0)]
    all_gather x1 -> x0, waiting for transfers between devices: 72 us -> none  [shards(): all_taps = lax.all_gather(filter_taps, 'seq', axis=0, tiled=True)]
    all_to_all x0 -> x1, starting transfers between devices: none -> 8.58 us  [shards(): lax.all_to_all(jnp.stack([filter_taps] * lax.axis_size('seq')), 'seq', 0, 0)]
    ppermute x15, starting transfers between devices: 74.8 us -> 81.1 us  [passed_along(): return lax.ppermute(block, axis, route)]
    another operation x0 -> x1, local copies, waits for them, and re-layouts: none -> 5.36 us  [shards(): jnp.stack([filter_taps] * lax.axis_size('seq'))]
  transfers between devices with their start and end apart: 17 -> 17, of which waited for: 17 -> 17; matrix products, arithmetic and copies ran while one was open for 15% -> 13% of each run, Pallas kernels for 0% -> 0%
where the time goes in v1:
time: 482 us; the launch traced here: 480 us
  waiting for transfers between devices  249 us (52%)
  starting transfers between devices  89.7 us (19%)
  matrix products  85.6 us (18%)
  local copies, waits for them, and re-layouts  20.5 us (4%)
  other arithmetic  20.1 us (4%)
  between operations  13.5 us (3%)
    all_to_all x1, waiting for transfers between devices, shards(): lax.all_to_all(jnp.stack([filter_taps] * lax.axis_size('seq')), 'seq', 0, 0)  114 us
    reduce_scatter x1, waiting for transfers between devices, shards(): lax.psum_scatter(lax.dot_general(out_proj, mixed_rows, (((1,), (1,)), (()...  96.7 us
    ppermute x15, starting transfers between devices, passed_along(): return lax.ppermute(block, axis, route)  81.1 us
    dot_general x32, matrix products, transform(): jnp.dot(tables[1], time_rows, preferred_element_type=jnp.float32)  39.4 us
    ppermute x15, waiting for transfers between devices, passed_along(): return lax.ppermute(block, axis, route)  38.5 us
    dot_general x32, matrix products, transform(): first = jnp.dot(tables[0], time_rows, preferred_element_type=jnp.float32)  33.5 us
    while x75, local copies, waits for them, and re-layouts  13.4 us
  transfers between devices with their start and end apart: 17, of which 17 were waited for; matrix products, arithmetic and copies ran while one was open for 13% of the time, Pallas kernels for 0%

profile of v1, /device:TPU:1, one launch (start us, length us, event | category | flops | bytes accessed | tf_op | source)
XLA Modules:
  0.0 479.9 jit_solution(17487459350677090651)
XLA Ops:
  6.5 5.4 %stack.2 = bf16[16,256,1024]{2,1,0:T(8,128)(2,1)} broadcast(bf16[256,1024]{1,0:T(8,128)(2,1)} %param.11), dimensions={1,2} | broadcast | bytes 8912896 | tf_op jit(solution)/shard_map/stack | solution.py:60
  11.9 8.6 %all-to-all-start = ((bf16[16,256,1024]{2,1,0:T(8,128)(2,1)}), bf16[16,256,1024]{2,1,0:T(8,128)(2,1)}, u32[]{:S(2)}, u32[]{:S(2)}) async-start(bf16[16,256,1024]{2,1,0:T(8,128)(2,1)} %stack.2), calls=%async_computation | async-start | bytes 16777216 | tf_op jit(solution)/shard_map/all_to_all | solution.py:60
  26.3 113.6 %all-to-all-done = bf16[16,256,1024]{2,1,0:T(8,128)(2,1)} async-done(((bf16[16,256,1024]{2,1,0:T(8,128)(2,1)}), bf16[16,256,1024]{2,1,0:T(8,128)(2,1)}, u32[]{:S(2)}, u32[]{:S(2)}) %all-to-all-start) | async-done | bytes 8388640 | tf_op jit(solution)/shard_map/all_to_all | solution.py:60
  144.5 219.0 %while.19 = (s32[]{:T(128)}, f32[512,1024]{1,0:T(8,128)S(1)}, f32[512,1024]{1,0:T(8,128)}, bf16[256,1024]{1,0:T(8,128)(2,1)}, bf16[4096,1024]{1,0:T(8,128)(2,1)}...) while((s32[]{:T(128)}, f32[512,1024]{1,0:T(8,128)S(1)}, ...), condition=%wide.region_1.2_spmd.clone.clone, body=%wide.region_0.1_spmd.clone.clone.sunk | while | flops 1079509760 | bytes 52436232 | solution.py:83
  144.7 9.9 %collective-permute-start = (bf16[256,1024]{1,0:T(8,128)(2,1)}, bf16[256,1024]{1,0:T(8,128)(2,1)S(1)}, u32[]{:S(2)}, u32[]{:S(2)}) collective-permute-start(bf16[256,1024]{1,0:T(8,128)(2,1)} %get-tuple-element.307), channel_id=1, source_target_pairs={{0,8},{8,16},{16,24},{24,32},{32,40},{40,48},{48,56},{56,64},{64,7... | collective-permute-start | bytes 1572872 | tf_op jit(solution)/shard_map/while/body/eval_jaxpr/ppermute | solution.py:11
  158.5 2.6 collective-permute-done
  163.8 4.3 collective-permute-start
  171.9 2.6 collective-permute-done
  177.2 4.3 collective-permute-start
  190.7 4.3 collective-permute-start
  204.2 4.3 collective-permute-start
  217.6 4.3 collective-permute-start
  231.1 4.3 collective-permute-start
  244.5 4.3 collective-permute-start
  258.0 4.3 collective-permute-start
  271.4 4.3 collective-permute-start
  284.9 4.3 collective-permute-start
  298.3 4.8 %collective-permute-start = (bf16[256,1024]{1,0:T(8,128)(2,1)}, bf16[256,1024]{1,0:T(8,128)(2,1)S(1)}, u32[]{:S(2)}, u32[]{:S(2)}) collective-permute-start(bf16[256,1024]{1,0:T(8,128)(2,1)} %get-tuple-element.307), channel_id=1, source_target_pairs={{0,8},{8,16},{16,24},{24,32},{32,40},{40,48},{48,56},{56,64},{64,7... | collective-permute-start | bytes 1572872 | tf_op jit(solution)/shard_map/while/body/eval_jaxpr/ppermute | solution.py:11
  312.3 7.9 %collective-permute-start = (bf16[256,1024]{1,0:T(8,128)(2,1)}, bf16[256,1024]{1,0:T(8,128)(2,1)S(1)}, u32[]{:S(2)}, u32[]{:S(2)}) collective-permute-start(bf16[256,1024]{1,0:T(8,128)(2,1)} %get-tuple-element.307), channel_id=1, source_target_pairs={{0,8},{8,16},{16,24},{24,32},{32,40},{40,48},{48,56},{56,64},{64,7... | collective-permute-start | bytes 1572872 | tf_op jit(solution)/shard_map/while/body/eval_jaxpr/ppermute | solution.py:11
  329.4 7.9 %collective-permute-start = (bf16[256,1024]{1,0:T(8,128)(2,1)}, bf16[256,1024]{1,0:T(8,128)(2,1)S(1)}, u32[]{:S(2)}, u32[]{:S(2)}) collective-permute-start(bf16[256,1024]{1,0:T(8,128)(2,1)} %get-tuple-element.307), channel_id=1, source_target_pairs={{0,8},{8,16},{16,24},{24,32},{32,40},{40,48},{48,56},{56,64},{64,7... | collective-permute-start | bytes 1572872 | tf_op jit(solution)/shard_map/while/body/eval_jaxpr/ppermute | solution.py:11
  346.5 7.9 %collective-permute-start = (bf16[256,1024]{1,0:T(8,128)(2,1)}, bf16[256,1024]{1,0:T(8,128)(2,1)S(1)}, u32[]{:S(2)}, u32[]{:S(2)}) collective-permute-start(bf16[256,1024]{1,0:T(8,128)(2,1)} %get-tuple-element.307), channel_id=1, source_target_pairs={{0,8},{8,16},{16,24},{24,32},{32,40},{40,48},{48,56},{56,64},{64,7... | collective-permute-start | bytes 1572872 | tf_op jit(solution)/shard_map/while/body/eval_jaxpr/ppermute | solution.py:11
  363.5 3.2 fusion.9
  366.8 9.5 %fusion.7 = bf16[8192,256]{0,1:T(8,128)(2,1)} fusion(bf16[256,1024]{1,0:T(8,128)(2,1)S(1)} %fusion.9, bf16[8192,1024]{1,0:T(8,128)(2,1)} %param.13), kind=kOutput, calls=%fused_computation.16 | convolution fusion | flops 4297064448 | bytes 21495808 | tf_op jit(solution)/shard_map/dot_general | solution.py:92
  376.3 96.7 %reduce-scatter.2.cloned.1.call-done = bf16[1024,256]{0,1:T(8,128)(2,1)} async-done(((bf16[8192,256]{0,1:T(8,128)(2,1)}), bf16[1024,256]{0,1:T(8,128)(2,1)}) %reduce-scatter.2.cloned.1.call-update) | async-done | bytes 524304 | tf_op jit(solution)/shard_map/reduce_scatter | solution.py:91
  (238 shorter events, 141.6 us)
Async XLA Ops:
  11.9 8.6 %copy-start.4 = (bf16[256,1024]{1,0:T(8,128)(2,1)S(1)}, bf16[256,1024]{1,0:T(8,128)(2,1)}, u32[]{:S(2)}) copy-start(bf16[256,1024]{1,0:T(8,128)(2,1)} %param.10) | copy-start | bytes 1572868
  11.9 8.6 %copy-start.5 = (bf16[256,1024]{1,0:T(8,128)(2,1)S(1)}, bf16[256,1024]{1,0:T(8,128)(2,1)}, u32[]{:S(2)}) copy-start(bf16[256,1024]{1,0:T(8,128)(2,1)} %param.9) | copy-start | bytes 1572868
  11.9 128.0 %all-to-all-start = ((bf16[16,256,1024]{2,1,0:T(8,128)(2,1)}), bf16[16,256,1024]{2,1,0:T(8,128)(2,1)}, u32[]{:S(2)}, u32[]{:S(2)}) async-start(bf16[16,256,1024]{2,1,0:T(8,128)(2,1)} %stack.2), calls=%async_computation | async-start | bytes 16777216 | tf_op jit(solution)/shard_map/all_to_all | solution.py:60
  20.5 452.5 %reduce-scatter.2.cloned.1.call-start = ((), (), s32[]{:S(2)}) async-start(), calls=%async_computation.2 | async-start | bytes 4718592 | tf_op jit(solution)/shard_map/reduce_scatter | solution.py:91
  20.7 5.1 %copy-start.3 = (bf16[256,1024]{1,0:T(8,128)(2,1)}, bf16[256,1024]{1,0:T(8,128)(2,1)S(1)}, u32[]{:S(2)}) copy-start(bf16[256,1024]{1,0:T(8,128)(2,1)S(1)} %multiply_convert_fusion) | copy-start | bytes 1572868
  144.5 219.1 %copy-start.6 = (f32[1024]{0:T(1024)S(1)}, f32[1024]{0:T(1024)}, u32[]{:S(2)}) copy-start(f32[1024]{0:T(1024)} %param.12) | copy-start | bytes 12292
  144.7 16.3 %collective-permute-start = (bf16[256,1024]{1,0:T(8,128)(2,1)}, bf16[256,1024]{1,0:T(8,128)(2,1)S(1)}, u32[]{:S(2)}, u32[]{:S(2)}) collective-permute-start(bf16[256,1024]{1,0:T(8,128)(2,1)} %get-tuple-element.307), channel_id=1, source_target_pairs={{0,8},{8,16},{16,24},{24,32},{32,40},{40,48},{48,56},{56,64},{64,7... | collective-permute-start | bytes 1572872 | tf_op jit(solution)/shard_map/while/body/eval_jaxpr/ppermute | solution.py:11
  158.4 3.5 copy-start.2
  163.8 10.7 %collective-permute-start = (bf16[256,1024]{1,0:T(8,128)(2,1)}, bf16[256,1024]{1,0:T(8,128)(2,1)S(1)}, u32[]{:S(2)}, u32[]{:S(2)}) collective-permute-start(bf16[256,1024]{1,0:T(8,128)(2,1)} %get-tuple-element.307), channel_id=1, source_target_pairs={{0,8},{8,16},{16,24},{24,32},{32,40},{40,48},{48,56},{56,64},{64,7... | collective-permute-start | bytes 1572872 | tf_op jit(solution)/shard_map/while/body/eval_jaxpr/ppermute | solution.py:11
  177.2 10.7 %collective-permute-start = (bf16[256,1024]{1,0:T(8,128)(2,1)}, bf16[256,1024]{1,0:T(8,128)(2,1)S(1)}, u32[]{:S(2)}, u32[]{:S(2)}) collective-permute-start(bf16[256,1024]{1,0:T(8,128)(2,1)} %get-tuple-element.307), channel_id=1, source_target_pairs={{0,8},{8,16},{16,24},{24,32},{32,40},{40,48},{48,56},{56,64},{64,7... | collective-permute-start | bytes 1572872 | tf_op jit(solution)/shard_map/while/body/eval_jaxpr/ppermute | solution.py:11
  185.4 3.5 copy-start.2
  190.7 10.7 %collective-permute-start = (bf16[256,1024]{1,0:T(8,128)(2,1)}, bf16[256,1024]{1,0:T(8,128)(2,1)S(1)}, u32[]{:S(2)}, u32[]{:S(2)}) collective-permute-start(bf16[256,1024]{1,0:T(8,128)(2,1)} %get-tuple-element.307), channel_id=1, source_target_pairs={{0,8},{8,16},{16,24},{24,32},{32,40},{40,48},{48,56},{56,64},{64,7... | collective-permute-start | bytes 1572872 | tf_op jit(solution)/shard_map/while/body/eval_jaxpr/ppermute | solution.py:11
  198.8 3.5 copy-start.2
  204.2 10.7 %collective-permute-start = (bf16[256,1024]{1,0:T(8,128)(2,1)}, bf16[256,1024]{1,0:T(8,128)(2,1)S(1)}, u32[]{:S(2)}, u32[]{:S(2)}) collective-permute-start(bf16[256,1024]{1,0:T(8,128)(2,1)} %get-tuple-element.307), channel_id=1, source_target_pairs={{0,8},{8,16},{16,24},{24,32},{32,40},{40,48},{48,56},{56,64},{64,7... | collective-permute-start | bytes 1572872 | tf_op jit(solution)/shard_map/while/body/eval_jaxpr/ppermute | solution.py:11
  217.6 10.7 %collective-permute-start = (bf16[256,1024]{1,0:T(8,128)(2,1)}, bf16[256,1024]{1,0:T(8,128)(2,1)S(1)}, u32[]{:S(2)}, u32[]{:S(2)}) collective-permute-start(bf16[256,1024]{1,0:T(8,128)(2,1)} %get-tuple-element.307), channel_id=1, source_target_pairs={{0,8},{8,16},{16,24},{24,32},{32,40},{40,48},{48,56},{56,64},{64,7... | collective-permute-start | bytes 1572872 | tf_op jit(solution)/shard_map/while/body/eval_jaxpr/ppermute | solution.py:11
  231.1 10.7 %collective-permute-start = (bf16[256,1024]{1,0:T(8,128)(2,1)}, bf16[256,1024]{1,0:T(8,128)(2,1)S(1)}, u32[]{:S(2)}, u32[]{:S(2)}) collective-permute-start(bf16[256,1024]{1,0:T(8,128)(2,1)} %get-tuple-element.307), channel_id=1, source_target_pairs={{0,8},{8,16},{16,24},{24,32},{32,40},{40,48},{48,56},{56,64},{64,7... | collective-permute-start | bytes 1572872 | tf_op jit(solution)/shard_map/while/body/eval_jaxpr/ppermute | solution.py:11
  244.5 10.7 %collective-permute-start = (bf16[256,1024]{1,0:T(8,128)(2,1)}, bf16[256,1024]{1,0:T(8,128)(2,1)S(1)}, u32[]{:S(2)}, u32[]{:S(2)}) collective-permute-start(bf16[256,1024]{1,0:T(8,128)(2,1)} %get-tuple-element.307), channel_id=1, source_target_pairs={{0,8},{8,16},{16,24},{24,32},{32,40},{40,48},{48,56},{56,64},{64,7... | collective-permute-start | bytes 1572872 | tf_op jit(solution)/shard_map/while/body/eval_jaxpr/ppermute | solution.py:11
  258.0 10.7 %collective-permute-start = (bf16[256,1024]{1,0:T(8,128)(2,1)}, bf16[256,1024]{1,0:T(8,128)(2,1)S(1)}, u32[]{:S(2)}, u32[]{:S(2)}) collective-permute-start(bf16[256,1024]{1,0:T(8,128)(2,1)} %get-tuple-element.307), channel_id=1, source_target_pairs={{0,8},{8,16},{16,24},{24,32},{32,40},{40,48},{48,56},{56,64},{64,7... | collective-permute-start | bytes 1572872 | tf_op jit(solution)/shard_map/while/body/eval_jaxpr/ppermute | solution.py:11
  271.4 10.7 %collective-permute-start = (bf16[256,1024]{1,0:T(8,128)(2,1)}, bf16[256,1024]{1,0:T(8,128)(2,1)S(1)}, u32[]{:S(2)}, u32[]{:S(2)}) collective-permute-start(bf16[256,1024]{1,0:T(8,128)(2,1)} %get-tuple-element.307), channel_id=1, source_target_pairs={{0,8},{8,16},{16,24},{24,32},{32,40},{40,48},{48,56},{56,64},{64,7... | collective-permute-start | bytes 1572872 | tf_op jit(solution)/shard_map/while/body/eval_jaxpr/ppermute | solution.py:11
  284.9 10.7 %collective-permute-start = (bf16[256,1024]{1,0:T(8,128)(2,1)}, bf16[256,1024]{1,0:T(8,128)(2,1)S(1)}, u32[]{:S(2)}, u32[]{:S(2)}) collective-permute-start(bf16[256,1024]{1,0:T(8,128)(2,1)} %get-tuple-element.307), channel_id=1, source_target_pairs={{0,8},{8,16},{16,24},{24,32},{32,40},{40,48},{48,56},{56,64},{64,7... | collective-permute-start | bytes 1572872 | tf_op jit(solution)/shard_map/while/body/eval_jaxpr/ppermute | solution.py:11
  298.3 11.2 %collective-permute-start = (bf16[256,1024]{1,0:T(8,128)(2,1)}, bf16[256,1024]{1,0:T(8,128)(2,1)S(1)}, u32[]{:S(2)}, u32[]{:S(2)}) collective-permute-start(bf16[256,1024]{1,0:T(8,128)(2,1)} %get-tuple-element.307), channel_id=1, source_target_pairs={{0,8},{8,16},{16,24},{24,32},{32,40},{40,48},{48,56},{56,64},{64,7... | collective-permute-start | bytes 1572872 | tf_op jit(solution)/shard_map/while/body/eval_jaxpr/ppermute | solution.py:11
  312.3 14.3 %collective-permute-start = (bf16[256,1024]{1,0:T(8,128)(2,1)}, bf16[256,1024]{1,0:T(8,128)(2,1)S(1)}, u32[]{:S(2)}, u32[]{:S(2)}) collective-permute-start(bf16[256,1024]{1,0:T(8,128)(2,1)} %get-tuple-element.307), channel_id=1, source_target_pairs={{0,8},{8,16},{16,24},{24,32},{32,40},{40,48},{48,56},{56,64},{64,7... | collective-permute-start | bytes 1572872 | tf_op jit(solution)/shard_map/while/body/eval_jaxpr/ppermute | solution.py:11
  329.4 14.3 %collective-permute-start = (bf16[256,1024]{1,0:T(8,128)(2,1)}, bf16[256,1024]{1,0:T(8,128)(2,1)S(1)}, u32[]{:S(2)}, u32[]{:S(2)}) collective-permute-start(bf16[256,1024]{1,0:T(8,128)(2,1)} %get-tuple-element.307), channel_id=1, source_target_pairs={{0,8},{8,16},{16,24},{24,32},{32,40},{40,48},{48,56},{56,64},{64,7... | collective-permute-start | bytes 1572872 | tf_op jit(solution)/shard_map/while/body/eval_jaxpr/ppermute | solution.py:11
  346.5 14.3 %collective-permute-start = (bf16[256,1024]{1,0:T(8,128)(2,1)}, bf16[256,1024]{1,0:T(8,128)(2,1)S(1)}, u32[]{:S(2)}, u32[]{:S(2)}) collective-permute-start(bf16[256,1024]{1,0:T(8,128)(2,1)} %get-tuple-element.307), channel_id=1, source_target_pairs={{0,8},{8,16},{16,24},{24,32},{32,40},{40,48},{48,56},{56,64},{64,7... | collective-permute-start | bytes 1572872 | tf_op jit(solution)/shard_map/while/body/eval_jaxpr/ppermute | solution.py:11
  (28 other events, 69.7 us)
Sparse Core Ops, SparseCore 0:
  376.4 96.5 reduce-scatter.1
